TPU v7x, 32 devices: a whole 2x2x4 slice. The times are simulated.
32 devices in a mesh: space: 8 (over z, x), kern: 4 (over y, core).
Axes of the slice: x: 2, y: 2, z: 4, core: 2. Of those that a mesh axis runs over, the one named last changes fastest.
Arguments:
- mask: bfloat16 [4096, 4096], P('space'), may hold values from -1 to 1
- kernels: float32 [2, 16, 512, 512], P(None, 'kern', 'space'), may hold values from -4 to 4
- target: int32 [1024, 1024], P('space'), may hold values 0 or 1
Outputs:
- gradient: float32 [4096, 4096], P('space')
- resist: float32 [1024, 1024], P('space')
All inputs are finite; a program needn't handle non-finite values. No bound on the sum of `target` on one device may be relied on, other than what follows from the above.
Results may differ from a plain program's by a relative error of at most 0.0003.
Values sent between devices are 32-bit elements; how exact they have to be, the bound alone decides.
A program may use at most 64 MiB of HBM per device.

v0:
```python
import jax
import jax.numpy as jnp
from jax import lax
from jax.sharding import PartitionSpec as P

N = 4096
B = 512
G = 1024
steepness = 8.0
threshold = 1.5
highest = lax.Precision.HIGHEST
block_limit = 1024


def phases(left, right, modulus):
    product = left[:, None] * right[None, :] % modulus
    return product.astype(jnp.float32) * (2.0 * jnp.pi / modulus)


def column_table(pixels, frequency, length):
    angle = phases(pixels, frequency, length)
    return jnp.concatenate([jnp.cos(angle), -jnp.sin(angle)], axis=1)


def row_table(pixels, frequency, length):
    angle = phases(pixels, frequency, length)
    return jnp.concatenate([jnp.cos(angle), -jnp.sin(angle)], axis=1) / length


def grid_table(frequency, points):
    angle = phases(frequency, jnp.arange(points, dtype=jnp.int32), points)
    return jnp.concatenate([jnp.cos(angle), jnp.sin(angle)], axis=1)


def forward_columns(mask, frequency):
    rows = mask.shape[0]
    span = min(block_limit, N)
    count = frequency.shape[0]

    def step(index, running):
        start = index * span
        table = column_table(start + jnp.arange(span, dtype=jnp.int32), frequency, N)
        piece = lax.dynamic_slice_in_dim(mask, start, span, 1).astype(jnp.float32)
        return running + lax.dot_general(table, piece, (((0,), (1,)), ((), ())), precision=highest)

    running = lax.fori_loop(0, N // span, step, jnp.zeros((2 * count, rows), jnp.float32))
    return running.reshape(2, count, rows)


def forward_rows(arrived):
    count = arrived.shape[1]
    flat = arrived.reshape(2 * count, N)
    frequency = jnp.arange(B, dtype=jnp.int32) - B // 2
    span = min(block_limit, N)

    def step(index, running):
        start = index * span
        table = row_table(start + jnp.arange(span, dtype=jnp.int32), frequency, N)
        piece = lax.dynamic_slice_in_dim(flat, start, span, 1)
        return running + jnp.dot(piece, table, precision=highest)

    running = lax.fori_loop(0, N // span, step, jnp.zeros((2 * count, 2 * B), jnp.float32))
    real_part = running[:count, :B] - running[count:, B:]
    imag_part = running[:count, B:] + running[count:, :B]
    return jnp.stack([real_part, imag_part])


def adjoint_rows(sum_re, sum_im):
    count = sum_re.shape[0]
    stacked = jnp.concatenate(
        [jnp.concatenate([sum_re, sum_im], axis=1), jnp.concatenate([sum_im, -sum_re], axis=1)],
        axis=0,
    )
    frequency = jnp.arange(B, dtype=jnp.int32) - B // 2
    span = min(block_limit, N)

    def step(index, output):
        start = index * span
        table = row_table(start + jnp.arange(span, dtype=jnp.int32), frequency, N)
        piece = lax.dot_general(stacked, table, (((1,), (1,)), ((), ())), precision=highest)
        return lax.dynamic_update_slice_in_dim(output, piece, start, 1)

    output = lax.fori_loop(0, N // span, step, jnp.zeros((2 * count, N), jnp.float32))
    return output.reshape(2, count, N)


def add_columns(total, spectrum, frequency):
    span = min(block_limit, N)

    def step(index, running):
        start = index * span
        table = column_table(start + jnp.arange(span, dtype=jnp.int32), frequency, N)
        piece = lax.dot_general(spectrum, table, (((0,), (1,)), ((), ())), precision=highest)
        current = lax.dynamic_slice_in_dim(running, start, span, 1)
        return lax.dynamic_update_slice_in_dim(running, current + piece, start, 1)

    return lax.fori_loop(0, N // span, step, total)


def local(mask, kernels, target):
    rows = mask.shape[0]
    kern_count = lax.axis_size("kern")
    space_count = lax.axis_size("space")
    group = lax.axis_index("kern")
    per_space = B // space_count
    per_group = per_space // kern_count
    frequency = jnp.arange(B, dtype=jnp.int32) - B // 2
    subset = (
        per_space * jnp.arange(space_count, dtype=jnp.int32)[:, None]
        + per_group * group
        + jnp.arange(per_group, dtype=jnp.int32)[None, :]
    )
    columns = forward_columns(mask, subset.reshape(-1) - B // 2)
    arrived = lax.all_to_all(columns, "space", split_axis=1, concat_axis=2, tiled=True)
    spectrum = lax.all_gather(forward_rows(arrived), "kern", axis=1, tiled=True)
    kern_swap = jnp.swapaxes(kernels, 1, 2)
    kernel_count = kern_swap.shape[2]
    spec_re = spectrum[0][:, None, :]
    spec_im = spectrum[1][:, None, :]
    prod_re = kern_swap[0] * spec_re - kern_swap[1] * spec_im
    prod_im = kern_swap[0] * spec_im + kern_swap[1] * spec_re
    grid = grid_table(frequency, G)
    lifted = jnp.dot(
        jnp.stack([prod_re, prod_im]).reshape(2 * per_space * kernel_count, B),
        grid,
        precision=highest,
    )
    lifted = lifted.reshape(2, per_space, kernel_count, 2 * G)
    coarse_re = lifted[0, :, :, :G] - lifted[1, :, :, G:]
    coarse_im = lifted[0, :, :, G:] + lifted[1, :, :, :G]
    coarse = jnp.stack([coarse_re, coarse_im], axis=1)
    gathered = lax.all_to_all(coarse, "space", split_axis=3, concat_axis=0, tiled=True)
    grid_rows = gathered.shape[3]
    image = lax.dot_general(
        gathered.reshape(B, 2 * kernel_count * grid_rows),
        grid,
        (((0,), (0,)), ((), ())),
        precision=highest,
    )
    image = image.reshape(2, kernel_count, grid_rows, 2 * G)
    field_re = image[0, :, :, :G] - image[1, :, :, G:]
    field_im = image[0, :, :, G:] + image[1, :, :, :G]
    partial_light = jnp.sum(field_re * field_re + field_im * field_im, axis=0) / (B * B)
    intensity = lax.psum(partial_light, "kern")
    resist = jax.nn.sigmoid(steepness * (intensity - threshold))
    slope = 2.0 * (resist - target.astype(jnp.float32)) * steepness * resist * (1.0 - resist)
    scale = 2.0 * slope / (B * B)
    grad_re = scale * field_re
    grad_im = scale * field_im
    mixed = jnp.stack(
        [
            jnp.concatenate([grad_re, grad_im], axis=-1),
            jnp.concatenate([grad_im, -grad_re], axis=-1),
        ]
    )
    mixed = mixed.reshape(2 * kernel_count * grid_rows, 2 * G)
    backward = lax.dot_general(grid, mixed, (((1,), (1,)), ((), ())), precision=highest)
    backward = backward.reshape(B, 2, kernel_count, grid_rows)
    returned = lax.all_to_all(backward, "space", split_axis=0, concat_axis=3, tiled=True)
    back_re = returned[:, 0]
    back_im = returned[:, 1]
    mixed_two = jnp.stack(
        [
            jnp.concatenate([back_re, back_im], axis=-1),
            jnp.concatenate([back_im, -back_re], axis=-1),
        ]
    )
    mixed_two = mixed_two.reshape(2 * per_space * kernel_count, 2 * G)
    spectral = lax.dot_general(mixed_two, grid, (((1,), (1,)), ((), ())), precision=highest)
    spectral = spectral.reshape(2, per_space, kernel_count, B)
    sum_re = jnp.sum(kern_swap[0] * spectral[0] + kern_swap[1] * spectral[1], axis=1)
    sum_im = jnp.sum(kern_swap[0] * spectral[1] - kern_swap[1] * spectral[0], axis=1)
    empty = jnp.zeros((rows, N), jnp.float32)
    shares = (
        lax.psum_scatter(sum_re, "kern", scatter_dimension=0, tiled=True),
        lax.psum_scatter(sum_im, "kern", scatter_dimension=0, tiled=True),
    )
    delta = adjoint_rows(shares[0], shares[1])
    landed = lax.all_to_all(delta, "space", split_axis=2, concat_axis=1, tiled=True)
    ordering = (
        per_group * jnp.arange(kern_count, dtype=jnp.int32)[:, None, None]
        + per_space * jnp.arange(space_count, dtype=jnp.int32)[None, :, None]
        + jnp.arange(per_group, dtype=jnp.int32)[None, None, :]
    )
    ordered_freq = ordering.reshape(-1) - B // 2
    piece = lax.all_gather(landed, "kern", axis=1, tiled=True)
    width = piece.shape[1]
    gradient = add_columns(empty, piece.reshape(2 * width, rows), ordered_freq)
    return (gradient, resist)


def solution(mesh):
    in_specs = (P("space", None), P(None, "kern", "space", None), P("space", None))
    out_specs = (P("space", None), P("space", None))
    return jax.shard_map(local, mesh=mesh, in_specs=in_specs, out_specs=out_specs, check_vma=False)
```

profile of v0, /device:TPU:0, one launch (start us, length us, event | category | flops | bytes accessed | tf_op | source)
XLA Modules:
  0.0 641.8 jit_solution(11022036640361063977)
XLA Ops:
  7.2 22.0 %while.66 = (s32[]{:T(128)}, f32[256,512]{1,0:T(8,128)S(1)}, bf16[512,4096]{1,0:T(8,128)(2,1)}, s32[8]{0:T(128)S(1)}, s32[]{:T(128)}, /*index=5*/s32[]{:T(128)}, s32[]{:T(128)}, s32[]{:T(128)}) while((s32[]{:T(128)}, f32[256,512]{1,0:T(8,128)S(1)}, bf16[512,4096]{1,0:T(8,128)(2,1)}, s32[8]{0:T(128)S(1)}, s32[]{:T(128)}, ...), condition=%wide.region_1.2_spmd.clone, body=%wide.region_0.1_spmd.clone.sunk | while | flops 1613104384 | bytes 4204733 | solution.py:46
  30.4 7.3 %all-to-all-start = ((f32[2,128,512]{2,0,1:T(2,128)}), f32[2,128,512]{2,0,1:T(2,128)S(1)}, u32[]{:S(2)}, u32[]{:S(2)}) async-start(f32[2,128,512]{2,0,1:T(2,128)} %copy.57), calls=%async_computation | async-start | bytes 1048576 | tf_op jit(solution)/shard_map/all_to_all | solution.py:114
  37.7 9.6 %fusion.78 = (f32[512,1024]{1,0:T(8,128)S(1)}, f32[512,1024]{1,0:T(8,128)}) fusion(s32[512]{0:T(512)S(1)} %iota_add_fusion.6), kind=kLoop, calls=%fused_computation.130 | loop fusion | flops 7340032 | bytes 4196352 | tf_op jit(solution)/shard_map/cos | solution.py:32
  47.3 4.8 all-to-all-done
  53.6 47.6 %while.67 = (s32[]{:T(128)}, f32[32,1024]{1,0:T(8,128)S(1)}, f32[32,4096]{1,0:T(8,128)}, s32[]{:T(128)}, s32[]{:T(128)}, /*index=5*/s32[]{:T(128)}, s32[]{:T(128)}) while((s32[]{:T(128)}, f32[32,1024]{1,0:T(8,128)S(1)}, f32[32,4096]{1,0:T(8,128)}, s32[]{:T(128)}, s32[]{:T(128)}, /*index=5*/s32[]{:T(128)}, s32[]{:T(128)}) %tuple.199), condition=%wide.region_3.4_spmd.clone, body=%wide.region_2.3_spmd.clone.sunk | while | flops 412681728 | bytes 8794261 | solution.py:62
  53.9 8.3 %fusion.116 = (f32[1024,512]{1,0:T(8,128)S(1)}, f32[1024,512]{1,0:T(8,128)S(1)}) fusion(s32[512]{0:T(512)S(1)} %iota_add_fusion.17, s32[1024]{0:T(1024)S(1)} %iota_add_fusion.18), kind=kLoop, calls=%fused_computation.79.clone.1 | loop fusion | flops 7864320 | bytes 4200448 | tf_op jit(solution)/shard_map/while/body/eval_jaxpr/cos | solution.py:27
  65.7 8.3 %fusion.116 = (f32[1024,512]{1,0:T(8,128)S(1)}, f32[1024,512]{1,0:T(8,128)S(1)}) fusion(s32[512]{0:T(512)S(1)} %iota_add_fusion.17, s32[1024]{0:T(1024)S(1)} %iota_add_fusion.18), kind=kLoop, calls=%fused_computation.79.clone.1 | loop fusion | flops 7864320 | bytes 4200448 | tf_op jit(solution)/shard_map/while/body/eval_jaxpr/cos | solution.py:27
  77.6 8.3 %fusion.116 = (f32[1024,512]{1,0:T(8,128)S(1)}, f32[1024,512]{1,0:T(8,128)S(1)}) fusion(s32[512]{0:T(512)S(1)} %iota_add_fusion.17, s32[1024]{0:T(1024)S(1)} %iota_add_fusion.18), kind=kLoop, calls=%fused_computation.79.clone.1 | loop fusion | flops 7864320 | bytes 4200448 | tf_op jit(solution)/shard_map/while/body/eval_jaxpr/cos | solution.py:27
  89.4 8.3 %fusion.116 = (f32[1024,512]{1,0:T(8,128)S(1)}, f32[1024,512]{1,0:T(8,128)S(1)}) fusion(s32[512]{0:T(512)S(1)} %iota_add_fusion.17, s32[1024]{0:T(1024)S(1)} %iota_add_fusion.18), kind=kLoop, calls=%fused_computation.79.clone.1 | loop fusion | flops 7864320 | bytes 4200448 | tf_op jit(solution)/shard_map/while/body/eval_jaxpr/cos | solution.py:27
  101.3 6.2 all_gather.6
  107.7 6.9 %fusion.61 = f32[2,64,4,2048]{3,1,2,0:T(8,128)S(1)} fusion(f32[512,1024]{1,0:T(8,128)S(1)} %copy-done.2, f32[512,1024]{1,0:T(8,128)S(1)} %get-tuple-element.572, f32[1,64,4,512]{3,1,2,0:T(8,128)S(1)} %get-tuple-element.563, f32[1,64,4,512]{3,1,2,0:T(8,128)S(1)} %get-tuple-element.562), kind=kOutput, calls=%fused_computation.97 | convolution fusion | flops 6443761664 | bytes 9437184 | tf_op jit(solution)/shard_map/dot_general | solution.py:123
  116.4 4.8 copy.60
  121.2 7.8 %reshape.172 = f32[8,1,65536]{2,1,0:T(1,128)} reshape(f32[1024,2,4,64]{3,2,1,0:T(4,128)} %bitcast.117) | data formatting | bytes 4194304
  129.0 53.8 %all_to_all.66 = f32[8,1,65536]{2,1,0:T(1,128)} all-to-all(f32[8,1,65536]{2,1,0:T(1,128)} %reshape.172), channel_id=1, replica_groups=mesh['space'=8,'kern'=4] {'space'}, dimensions={0} | all-to-all | bytes 4194304 | tf_op jit(solution)/shard_map/all_to_all | solution.py:132
  183.3 8.5 %reduce = f32[8,65536]{1,0:T(8,128)} reduce(f32[8,1,65536]{2,1,0:T(1,128)} %all_to_all.66, f32[]{:T(128)} %broadcast.375), dimensions={1}, to_apply=%all_to_all.51.reduce_sub_computation | reduce | bytes 4194308 | tf_op jit(solution)/shard_map/all_to_all | solution.py:132
  191.9 6.5 %reshape.173 = f32[1024,2,4,64]{3,2,1,0:T(4,128)} reshape(f32[8,65536]{1,0:T(8,128)} %reduce) | data formatting | bytes 4194304
  198.3 4.8 copy.61
  209.2 16.7 %fusion.59 = f32[2,4,128,2048]{3,2,1,0:T(8,128)S(1)} fusion(f32[2,4,128,512]{3,2,1,0:T(8,128)} %bitcast.122, f32[512,1024]{1,0:T(8,128)} %get-tuple-element.573, f32[512,1024]{1,0:T(8,128)S(1)} %get-tuple-element.572), kind=kOutput, calls=%fused_computation.95 | convolution fusion | flops 12885950464 | bytes 14680064 | tf_op jit(solution)/shard_map/dot_general | solution.py:134
  230.2 32.4 %all-reduce.2.cloned.1.call-done = f32[128,1024]{1,0:T(8,128)} async-done(((f32[128,1024]{1,0:T(8,128)}), f32[128,1024]{1,0:T(8,128)}) %all-reduce.2.cloned.1.call-update) | async-done | bytes 524304 | tf_op jit(solution)/shard_map/psum | solution.py:144
  264.8 4.5 fusion.88
  273.3 15.5 %fusion.54 = f32[512,2,4,128]{3,0,2,1:T(8,128)S(1)} fusion(f32[1,4,128,2048]{3,2,1,0:T(8,128)} %get-tuple-element.561, f32[1,4,128,2048]{3,2,1,0:T(8,128)} %get-tuple-element.560, f32[512,1024]{1,0:T(8,128)S(1)} %copy-done.3, f32[512,1024]{1,0:T(8,128)S(1)} %get-tuple-element.572), kind=kOutput, calls=%fused_computation.86 | convolution fusion | flops 12888047616 | bytes 14680064 | tf_op jit(solution)/shard_map/dot_general | solution.py:157
  290.1 53.1 %all_to_all.67 = f32[512,2,4,128]{3,2,1,0:T(4,128)S(1)} all-to-all(f32[512,2,4,128]{3,2,1,0:T(4,128)S(1)} %copy.63), channel_id=1, replica_groups=mesh['space'=8,'kern'=4] {'space'}, dimensions={0} | all-to-all | bytes 4194304 | tf_op jit(solution)/shard_map/all_to_all | solution.py:159
  351.5 4.7 copy.65
  356.2 5.3 reshape.168
  361.6 8.9 %fusion.71 = f32[512,512]{1,0:T(8,128)S(1)} fusion(f32[512,2048]{1,0:T(8,128)} %reshape.168, f32[512,1024]{1,0:T(8,128)} %get-tuple-element.573, f32[512,1024]{1,0:T(8,128)S(1)} %get-tuple-element.572), kind=kOutput, calls=%fused_computation.117 | convolution fusion | flops 6443499520 | bytes 9437184 | tf_op jit(solution)/shard_map/dot_general | solution.py:169
  372.8 17.0 %reduce-scatter.3.cloned.1.call-done = f32[16,512]{1,0:T(8,128)} async-done(((f32[64,512]{1,0:T(8,128)}), f32[16,512]{1,0:T(8,128)}) %reduce-scatter.3.cloned.1.call-update) | async-done | bytes 32784 | tf_op jit(solution)/shard_map/reduce_scatter | solution.py:175
  390.5 21.9 %reduce-scatter.5.cloned.1.call-done = f32[16,512]{1,0:T(8,128)} async-done(((f32[64,512]{1,0:T(8,128)}), f32[16,512]{1,0:T(8,128)}) %reduce-scatter.5.cloned.1.call-update) | async-done | bytes 32784 | tf_op jit(solution)/shard_map/reduce_scatter | solution.py:176
  413.3 49.2 %while.64 = (s32[]{:T(128)}, f32[32,4096]{1,0:T(8,128)S(1)}, f32[32,1024]{1,0:T(8,128)S(1)}, s32[]{:T(128)}, s32[]{:T(128)}, /*index=5*/s32[]{:T(128)}, s32[]{:T(128)}) while((s32[]{:T(128)}, f32[32,4096]{1,0:T(8,128)S(1)}, f32[32,1024]{1,0:T(8,128)S(1)}, s32[]{:T(128)}, s32[]{:T(128)}, /*index=5*/s32[]{:T(128)}, ...), condition=%wide.region_11.12_spmd.clone, body=%wide.region_10.11_spmd.clone.sunk | while | flops 412616192 | bytes 8663171 | solution.py:83
  413.5 8.3 %fusion.107 = (f32[1024,512]{1,0:T(8,128)S(1)}, f32[1024,512]{1,0:T(8,128)S(1)}) fusion(s32[512]{0:T(512)S(1)} %iota_add_fusion.13, s32[1024]{0:T(1024)S(1)} %iota_add_fusion.14), kind=kLoop, calls=%fused_computation.20.clone.1 | loop fusion | flops 7864320 | bytes 4200448 | tf_op jit(solution)/shard_map/while/body/eval_jaxpr/cos | solution.py:27
  425.8 8.3 %fusion.107 = (f32[1024,512]{1,0:T(8,128)S(1)}, f32[1024,512]{1,0:T(8,128)S(1)}) fusion(s32[512]{0:T(512)S(1)} %iota_add_fusion.13, s32[1024]{0:T(1024)S(1)} %iota_add_fusion.14), kind=kLoop, calls=%fused_computation.20.clone.1 | loop fusion | flops 7864320 | bytes 4200448 | tf_op jit(solution)/shard_map/while/body/eval_jaxpr/cos | solution.py:27
  438.0 8.3 %fusion.107 = (f32[1024,512]{1,0:T(8,128)S(1)}, f32[1024,512]{1,0:T(8,128)S(1)}) fusion(s32[512]{0:T(512)S(1)} %iota_add_fusion.13, s32[1024]{0:T(1024)S(1)} %iota_add_fusion.14), kind=kLoop, calls=%fused_computation.20.clone.1 | loop fusion | flops 7864320 | bytes 4200448 | tf_op jit(solution)/shard_map/while/body/eval_jaxpr/cos | solution.py:27
  450.3 8.3 %fusion.107 = (f32[1024,512]{1,0:T(8,128)S(1)}, f32[1024,512]{1,0:T(8,128)S(1)}) fusion(s32[512]{0:T(512)S(1)} %iota_add_fusion.13, s32[1024]{0:T(1024)S(1)} %iota_add_fusion.14), kind=kLoop, calls=%fused_computation.20.clone.1 | loop fusion | flops 7864320 | bytes 4200448 | tf_op jit(solution)/shard_map/while/body/eval_jaxpr/cos | solution.py:27
  462.5 4.3 copy.70
  466.8 7.4 %reshape.174 = f32[8,1,16384]{2,1,0:T(1,128)S(1)} reshape(f32[4096,2,16]{2,1,0:T(2,128)} %bitcast.119) | data formatting | bytes 1048576
  474.2 19.3 %all_to_all.68 = f32[8,1,16384]{2,1,0:T(1,128)S(1)} all-to-all(f32[8,1,16384]{2,1,0:T(1,128)S(1)} %reshape.174), channel_id=1, replica_groups=mesh['space'=8,'kern'=4] {'space'}, dimensions={0} | all-to-all | bytes 1048576 | tf_op jit(solution)/shard_map/all_to_all | solution.py:179
  495.4 7.6 %reshape.175 = f32[4096,2,16]{2,1,0:T(2,128)} reshape(f32[8,16384]{1,0:T(8,128)S(1)} %reduce.1) | data formatting | bytes 1048576
  503.0 6.3 copy.76
  509.4 20.8 %all-gather.2.cloned.1.call-done = f32[2,512,512]{2,1,0:T(8,128)} async-done(((f32[2,128,512]{2,1,0:T(8,128)}), f32[2,512,512]{2,1,0:T(8,128)}) %all-gather.2.cloned.1.call-update) | async-done | bytes 2097168 | tf_op jit(solution)/shard_map/all_gather | solution.py:186
  530.2 4.4 broadcast_in_dim.45.clone
  534.6 100.2 %while.65 = (s32[]{:T(128)}, f32[512,4096]{1,0:T(8,128)}, f32[1024,512]{1,0:T(8,128)}, s32[4,8]{1,0:T(4,128)S(1)}, s32[]{:T(128)}, /*index=5*/s32[]{:T(128)}, s32[]{:T(128)}, s32[]{:T(128)}) while((s32[]{:T(128)}, f32[512,4096]{1,0:T(8,128)}, f32[1024,512]{1,0:T(8,128)}, s32[4,8]{1,0:T(4,128)S(1)}, s32[]{:T(128)}, ...), condition=%wide.region_13.14_spmd.clone, body=%wide.region_12.13_spmd.clone.sunk | while | flops 6451890176 | bytes 39862572 | solution.py:97
  540.2 8.3 %fusion.111 = (f32[1024,512]{1,0:T(8,128)S(1)}, f32[1024,512]{1,0:T(8,128)S(1)}) fusion(s32[512]{0:T(512)S(1)} %sub.133, s32[1024]{0:T(1024)S(1)} %iota_add_fusion.15), kind=kLoop, calls=%fused_computation.39.clone.1 | loop fusion | flops 7864320 | bytes 4200448 | tf_op jit(solution)/shard_map/while/body/eval_jaxpr/cos | solution.py:22
  548.5 8.0 %bitcast_add_fusion.2 = f32[512,1024]{0,1:T(8,128)} fusion(f32[512,1024]{0,1:T(8,128)S(1)} %copy.92, f32[1024,512]{1,0:T(8,128)S(1)} %copy-done.1, f32[1024,512]{1,0:T(8,128)S(1)} %get-tuple-element.665, f32[1024,512]{1,0:T(8,128)S(1)} %get-tuple-element.666), kind=kOutput, calls=%fused_computation.37.clone.1 | convolution fusion | flops 6444023808 | bytes 10485760 | tf_op jit(solution)/shard_map/while/body/eval_jaxpr/dot_general | solution.py:93
  565.1 8.3 %fusion.111 = (f32[1024,512]{1,0:T(8,128)S(1)}, f32[1024,512]{1,0:T(8,128)S(1)}) fusion(s32[512]{0:T(512)S(1)} %sub.133, s32[1024]{0:T(1024)S(1)} %iota_add_fusion.15), kind=kLoop, calls=%fused_computation.39.clone.1 | loop fusion | flops 7864320 | bytes 4200448 | tf_op jit(solution)/shard_map/while/body/eval_jaxpr/cos | solution.py:22
  573.4 8.0 %bitcast_add_fusion.2 = f32[512,1024]{0,1:T(8,128)} fusion(f32[512,1024]{0,1:T(8,128)S(1)} %copy.92, f32[1024,512]{1,0:T(8,128)S(1)} %copy-done.1, f32[1024,512]{1,0:T(8,128)S(1)} %get-tuple-element.665, f32[1024,512]{1,0:T(8,128)S(1)} %get-tuple-element.666), kind=kOutput, calls=%fused_computation.37.clone.1 | convolution fusion | flops 6444023808 | bytes 10485760 | tf_op jit(solution)/shard_map/while/body/eval_jaxpr/dot_general | solution.py:93
  590.1 8.3 %fusion.111 = (f32[1024,512]{1,0:T(8,128)S(1)}, f32[1024,512]{1,0:T(8,128)S(1)}) fusion(s32[512]{0:T(512)S(1)} %sub.133, s32[1024]{0:T(1024)S(1)} %iota_add_fusion.15), kind=kLoop, calls=%fused_computation.39.clone.1 | loop fusion | flops 7864320 | bytes 4200448 | tf_op jit(solution)/shard_map/while/body/eval_jaxpr/cos | solution.py:22
  598.4 8.0 %bitcast_add_fusion.2 = f32[512,1024]{0,1:T(8,128)} fusion(f32[512,1024]{0,1:T(8,128)S(1)} %copy.92, f32[1024,512]{1,0:T(8,128)S(1)} %copy-done.1, f32[1024,512]{1,0:T(8,128)S(1)} %get-tuple-element.665, f32[1024,512]{1,0:T(8,128)S(1)} %get-tuple-element.666), kind=kOutput, calls=%fused_computation.37.clone.1 | convolution fusion | flops 6444023808 | bytes 10485760 | tf_op jit(solution)/shard_map/while/body/eval_jaxpr/dot_general | solution.py:93
  615.1 8.3 %fusion.111 = (f32[1024,512]{1,0:T(8,128)S(1)}, f32[1024,512]{1,0:T(8,128)S(1)}) fusion(s32[512]{0:T(512)S(1)} %sub.133, s32[1024]{0:T(1024)S(1)} %iota_add_fusion.15), kind=kLoop, calls=%fused_computation.39.clone.1 | loop fusion | flops 7864320 | bytes 4200448 | tf_op jit(solution)/shard_map/while/body/eval_jaxpr/cos | solution.py:22
  623.4 8.0 %bitcast_add_fusion.2 = f32[512,1024]{0,1:T(8,128)} fusion(f32[512,1024]{0,1:T(8,128)S(1)} %copy.92, f32[1024,512]{1,0:T(8,128)S(1)} %copy-done.1, f32[1024,512]{1,0:T(8,128)S(1)} %get-tuple-element.665, f32[1024,512]{1,0:T(8,128)S(1)} %get-tuple-element.666), kind=kOutput, calls=%fused_computation.37.clone.1 | convolution fusion | flops 6444023808 | bytes 10485760 | tf_op jit(solution)/shard_map/while/body/eval_jaxpr/dot_general | solution.py:93
  (137 shorter events, 123.4 us)
Async XLA Ops:
  30.4 21.7 %all-to-all-start = ((f32[2,128,512]{2,0,1:T(2,128)}), f32[2,128,512]{2,0,1:T(2,128)S(1)}, u32[]{:S(2)}, u32[]{:S(2)}) async-start(f32[2,128,512]{2,0,1:T(2,128)} %copy.57), calls=%async_computation | async-start | bytes 1048576 | tf_op jit(solution)/shard_map/all_to_all | solution.py:114
  37.6 225.0 %all-reduce.2.cloned.1.call-start = ((), (), s32[]{:S(2)}) async-start(), calls=%async_computation.6 | async-start | bytes 1048576 | tf_op jit(solution)/shard_map/psum | solution.py:144
  53.6 53.8 %copy-start.5 = (f32[2,4,64,512]{3,2,1,0:T(8,128)S(1)}, f32[2,4,64,512]{3,2,1,0:T(8,128)}, u32[]{:S(2)}) copy-start(f32[2,4,64,512]{3,2,1,0:T(8,128)} %param.12) | copy-start | bytes 3145732
  101.2 6.5 %copy-start.2 = (f32[512,1024]{1,0:T(8,128)S(1)}, f32[512,1024]{1,0:T(8,128)}, u32[]{:S(2)}) copy-start(f32[512,1024]{1,0:T(8,128)} %get-tuple-element.573) | copy-start | bytes 6291460
  225.9 3.4 copy-start
  230.2 159.6 %reduce-scatter.3.cloned.1.call-start = ((), (), s32[]{:S(2)}) async-start(), calls=%async_computation.7 | async-start | bytes 163840 | tf_op jit(solution)/shard_map/reduce_scatter | solution.py:175
  269.3 4.0 copy-start.3
  348.5 1.9 copy-start.4
  372.0 40.5 %reduce-scatter.5.cloned.1.call-start = ((), (), s32[]{:S(2)}) async-start(), calls=%async_computation.8 | async-start | bytes 163840 | tf_op jit(solution)/shard_map/reduce_scatter | solution.py:176
  372.7 157.5 %all-gather.2.cloned.1.call-start = ((), (), s32[]{:S(2)}) async-start(), calls=%async_computation.9 | async-start | bytes 2621440 | tf_op jit(solution)/shard_map/all_gather | solution.py:186
  540.1 8.3 %copy-start.1 = (f32[1024,512]{1,0:T(8,128)S(1)}, f32[1024,512]{1,0:T(8,128)}, u32[]{:S(2)}) copy-start(f32[1024,512]{1,0:T(8,128)} %get-tuple-element.762) | copy-start | bytes 6291460 | tf_op jit(solution)/shard_map/while
  565.1 8.3 %copy-start.1 = (f32[1024,512]{1,0:T(8,128)S(1)}, f32[1024,512]{1,0:T(8,128)}, u32[]{:S(2)}) copy-start(f32[1024,512]{1,0:T(8,128)} %get-tuple-element.762) | copy-start | bytes 6291460 | tf_op jit(solution)/shard_map/while
  590.1 8.3 %copy-start.1 = (f32[1024,512]{1,0:T(8,128)S(1)}, f32[1024,512]{1,0:T(8,128)}, u32[]{:S(2)}) copy-start(f32[1024,512]{1,0:T(8,128)} %get-tuple-element.762) | copy-start | bytes 6291460 | tf_op jit(solution)/shard_map/while
  615.1 8.3 %copy-start.1 = (f32[1024,512]{1,0:T(8,128)S(1)}, f32[1024,512]{1,0:T(8,128)}, u32[]{:S(2)}) copy-start(f32[1024,512]{1,0:T(8,128)} %get-tuple-element.762) | copy-start | bytes 6291460 | tf_op jit(solution)/shard_map/while
Sparse Core Ops, SparseCore 0:
  230.3 32.2 all-reduce.1
  372.1 17.5 reduce-scatter.2
  392.9 19.5 reduce-scatter.4
  509.4 20.7 all-gather.1
where the time goes:
time: 649 us; the launch traced here: 642 us
  other arithmetic  149 us (23%)
  blocking collectives  132 us (20%)
  matrix products  122 us (19%)
  local copies, waits for them, and re-layouts  118 us (18%)
  waiting for transfers between devices  97.6 us (15%)
  between operations  14.5 us (2%)
  starting transfers between devices  7.41 us (1%)
    cos x8, other arithmetic, row_table(): return jnp.concatenate([jnp.cos(angle), -jnp.sin(angle)], axis=1) / length  66.3 us
    all_to_all x1, blocking collectives, local(): lax.all_to_all(coarse, 'space', split_axis=3, concat_axis=0, tiled=True)  53.8 us
    all_to_all x1, blocking collectives, local(): lax.all_to_all(backward, 'space', split_axis=0, concat_axis=3, tiled=True)  53.1 us
    cos x8, other arithmetic, column_table(): return jnp.concatenate([jnp.cos(angle), -jnp.sin(angle)], axis=1)  41.7 us
    unnamed x15, local copies, waits for them, and re-layouts  33.1 us
    psum x1, waiting for transfers between devices, local(): intensity = lax.psum(partial_light, 'kern')  32.4 us
    dot_general x4, matrix products, step(): lax.dot_general(spectrum, table, (((0,), (1,)), ((), ())), precision=high...  32.1 us
    reduce_scatter x1, waiting for transfers between devices, local(): lax.psum_scatter(sum_im, 'kern', scatter_dimension=0, tiled=True)  21.9 us
  transfers between devices with their start and end apart: 5, of which 5 were waited for; matrix products, arithmetic and copies ran while one was open for 2% of the time, Pallas kernels for 0%

commit v1 on v0

--- a/solution.py
+++ b/solution.py
@@ -141,7 +141,13 @@
     field_re = image[0, :, :, :G] - image[1, :, :, G:]
     field_im = image[0, :, :, G:] + image[1, :, :, :G]
     partial_light = jnp.sum(field_re * field_re + field_im * field_im, axis=0) / (B * B)
-    intensity = lax.psum(partial_light, "kern")
+    count_2 = lax.axis_size("kern")
+    intensity, reach = (partial_light, 1)
+    while reach < count_2:
+        intensity = intensity + lax.ppermute(
+            intensity, "kern", [(i, i ^ reach) for i in range(count_2)]
+        )
+        reach = 2 * reach
     resist = jax.nn.sigmoid(steepness * (intensity - threshold))
     slope = 2.0 * (resist - target.astype(jnp.float32)) * steepness * resist * (1.0 - resist)
     scale = 2.0 * slope / (B * B)

time: 649 us -> 624 us (0.961)
  waiting for transfers between devices: 97.6 us -> 80.5 us
    psum x1 -> x0, waiting for transfers between devices: 32.4 us -> none  [local(): intensity = lax.psum(partial_light, 'kern')]
    ppermute x0 -> x2, waiting for transfers between devices: none -> 14.3 us  [local(): lax.ppermute(intensity, 'kern', [(i, i ^ reach) for i in range(count_2)])]
  transfers between devices with their start and end apart: 5 -> 6, of which waited for: 5 -> 6; matrix products, arithmetic and copies ran while one was open for 2% -> 2% of each run, Pallas kernels for 0% -> 0%
where the time goes in v1:
time: 624 us; the launch traced here: 617 us
  other arithmetic  144 us (23%)
  blocking collectives  131 us (21%)
  matrix products  121 us (19%)
  local copies, waits for them, and re-layouts  115 us (18%)
  waiting for transfers between devices  80.5 us (13%)
  between operations  14.5 us (2%)
  starting transfers between devices  9.02 us (1%)
    cos x8, other arithmetic, row_table(): return jnp.concatenate([jnp.cos(angle), -jnp.sin(angle)], axis=1) / length  66.3 us
    all_to_all x1, blocking collectives, local(): lax.all_to_all(coarse, 'space', split_axis=3, concat_axis=0, tiled=True)  53.8 us
    all_to_all x1, blocking collectives, local(): lax.all_to_all(backward, 'space', split_axis=0, concat_axis=3, tiled=True)  51.6 us
    cos x8, other arithmetic, column_table(): return jnp.concatenate([jnp.cos(angle), -jnp.sin(angle)], axis=1)  41.7 us
    dot_general x4, matrix products, step(): lax.dot_general(spectrum, table, (((0,), (1,)), ((), ())), precision=high...  32 us
    unnamed x15, local copies, waits for them, and re-layouts  30.9 us
    reduce_scatter x1, waiting for transfers between devices, local(): lax.psum_scatter(sum_im, 'kern', scatter_dimension=0, tiled=True)  22 us
    all_gather x1, waiting for transfers between devices, local(): piece = lax.all_gather(landed, 'kern', axis=1, tiled=True)  20.8 us
  transfers between devices with their start and end apart: 6, of which 6 were waited for; matrix products, arithmetic and copies ran while one was open for 2% of the time, Pallas kernels for 0%

profile of v1, /device:TPU:0, one launch (start us, length us, event | category | flops | bytes accessed | tf_op | source)
XLA Modules:
  0.0 616.9 jit_solution(5234536926072791631)
XLA Ops:
  7.2 22.0 %while.66 = (s32[]{:T(128)}, f32[256,512]{1,0:T(8,128)S(1)}, bf16[512,4096]{1,0:T(8,128)(2,1)}, s32[8]{0:T(128)S(1)}, s32[]{:T(128)}, /*index=5*/s32[]{:T(128)}, s32[]{:T(128)}, s32[]{:T(128)}) while((s32[]{:T(128)}, f32[256,512]{1,0:T(8,128)S(1)}, bf16[512,4096]{1,0:T(8,128)(2,1)}, s32[8]{0:T(128)S(1)}, s32[]{:T(128)}, ...), condition=%wide.region_1.2_spmd.clone, body=%wide.region_0.1_spmd.clone.sunk | while | flops 1613104384 | bytes 4204733 | solution.py:46
  30.4 7.3 %all-to-all-start = ((f32[2,128,512]{2,0,1:T(2,128)}), f32[2,128,512]{2,0,1:T(2,128)S(1)}, u32[]{:S(2)}, u32[]{:S(2)}) async-start(f32[2,128,512]{2,0,1:T(2,128)} %copy.57), calls=%async_computation | async-start | bytes 1048576 | tf_op jit(solution)/shard_map/all_to_all | solution.py:114
  37.7 9.6 %fusion.78 = (f32[512,1024]{1,0:T(8,128)S(1)}, f32[512,1024]{1,0:T(8,128)}) fusion(s32[512]{0:T(512)S(1)} %iota_add_fusion.6), kind=kLoop, calls=%fused_computation.130 | loop fusion | flops 7340032 | bytes 4196352 | tf_op jit(solution)/shard_map/cos | solution.py:32
  47.3 4.8 all-to-all-done
  53.6 47.6 %while.67 = (s32[]{:T(128)}, f32[32,1024]{1,0:T(8,128)S(1)}, f32[32,4096]{1,0:T(8,128)}, s32[]{:T(128)}, s32[]{:T(128)}, /*index=5*/s32[]{:T(128)}, s32[]{:T(128)}) while((s32[]{:T(128)}, f32[32,1024]{1,0:T(8,128)S(1)}, f32[32,4096]{1,0:T(8,128)}, s32[]{:T(128)}, s32[]{:T(128)}, /*index=5*/s32[]{:T(128)}, s32[]{:T(128)}) %tuple.197), condition=%wide.region_3.4_spmd.clone, body=%wide.region_2.3_spmd.clone.sunk | while | flops 412681728 | bytes 8794261 | solution.py:62
  53.9 8.3 %fusion.117 = (f32[1024,512]{1,0:T(8,128)S(1)}, f32[1024,512]{1,0:T(8,128)S(1)}) fusion(s32[512]{0:T(512)S(1)} %iota_add_fusion.17, s32[1024]{0:T(1024)S(1)} %iota_add_fusion.18), kind=kLoop, calls=%fused_computation.79.clone.1 | loop fusion | flops 7864320 | bytes 4200448 | tf_op jit(solution)/shard_map/while/body/eval_jaxpr/cos | solution.py:27
  65.7 8.3 %fusion.117 = (f32[1024,512]{1,0:T(8,128)S(1)}, f32[1024,512]{1,0:T(8,128)S(1)}) fusion(s32[512]{0:T(512)S(1)} %iota_add_fusion.17, s32[1024]{0:T(1024)S(1)} %iota_add_fusion.18), kind=kLoop, calls=%fused_computation.79.clone.1 | loop fusion | flops 7864320 | bytes 4200448 | tf_op jit(solution)/shard_map/while/body/eval_jaxpr/cos | solution.py:27
  77.6 8.3 %fusion.117 = (f32[1024,512]{1,0:T(8,128)S(1)}, f32[1024,512]{1,0:T(8,128)S(1)}) fusion(s32[512]{0:T(512)S(1)} %iota_add_fusion.17, s32[1024]{0:T(1024)S(1)} %iota_add_fusion.18), kind=kLoop, calls=%fused_computation.79.clone.1 | loop fusion | flops 7864320 | bytes 4200448 | tf_op jit(solution)/shard_map/while/body/eval_jaxpr/cos | solution.py:27
  89.4 8.3 %fusion.117 = (f32[1024,512]{1,0:T(8,128)S(1)}, f32[1024,512]{1,0:T(8,128)S(1)}) fusion(s32[512]{0:T(512)S(1)} %iota_add_fusion.17, s32[1024]{0:T(1024)S(1)} %iota_add_fusion.18), kind=kLoop, calls=%fused_computation.79.clone.1 | loop fusion | flops 7864320 | bytes 4200448 | tf_op jit(solution)/shard_map/while/body/eval_jaxpr/cos | solution.py:27
  101.3 6.2 %all_gather.6 = f32[2,64,512]{2,1,0:T(8,128)S(1)} all-gather(f32[2,16,512]{2,1,0:T(8,128)S(1)} %pad_maximum_fusion.7), channel_id=1, replica_groups=mesh['space'=8,'kern'=4] {'kern'}, dimensions={1}, use_global_device_ids=true | all-gather | bytes 327680 | tf_op jit(solution)/shard_map/all_gather | solution.py:115
  107.7 6.9 %fusion.61 = f32[2,64,4,2048]{3,1,2,0:T(8,128)S(1)} fusion(f32[512,1024]{1,0:T(8,128)S(1)} %copy-done.1, f32[512,1024]{1,0:T(8,128)S(1)} %get-tuple-element.572, f32[1,64,4,512]{3,1,2,0:T(8,128)S(1)} %get-tuple-element.563, f32[1,64,4,512]{3,1,2,0:T(8,128)S(1)} %get-tuple-element.562), kind=kOutput, calls=%fused_computation.97 | convolution fusion | flops 6443761664 | bytes 9437184 | tf_op jit(solution)/shard_map/dot_general | solution.py:123
  116.4 4.8 copy.60
  121.2 7.8 %reshape.172 = f32[8,1,65536]{2,1,0:T(1,128)} reshape(f32[1024,2,4,64]{3,2,1,0:T(4,128)} %bitcast.117) | data formatting | bytes 4194304
  129.0 53.8 %all_to_all.66 = f32[8,1,65536]{2,1,0:T(1,128)} all-to-all(f32[8,1,65536]{2,1,0:T(1,128)} %reshape.172), channel_id=1, replica_groups=mesh['space'=8,'kern'=4] {'space'}, dimensions={0} | all-to-all | bytes 4194304 | tf_op jit(solution)/shard_map/all_to_all | solution.py:132
  183.3 8.5 %reduce = f32[8,65536]{1,0:T(8,128)} reduce(f32[8,1,65536]{2,1,0:T(1,128)} %all_to_all.66, f32[]{:T(128)} %broadcast.377), dimensions={1}, to_apply=%all_to_all.51.reduce_sub_computation | reduce | bytes 4194308 | tf_op jit(solution)/shard_map/all_to_all | solution.py:132
  191.8 6.5 %reshape.173 = f32[1024,2,4,64]{3,2,1,0:T(4,128)} reshape(f32[8,65536]{1,0:T(8,128)} %reduce) | data formatting | bytes 4194304
  198.3 4.8 copy.61
  209.2 15.8 %fusion.59 = f32[2,4,128,2048]{3,2,1,0:T(8,128)S(1)} fusion(f32[2,4,128,512]{3,2,1,0:T(8,128)} %bitcast.122, f32[512,1024]{1,0:T(8,128)} %get-tuple-element.573, f32[512,1024]{1,0:T(8,128)S(1)} %get-tuple-element.572), kind=kOutput, calls=%fused_computation.95 | convolution fusion | flops 12885950464 | bytes 14680064 | tf_op jit(solution)/shard_map/dot_general | solution.py:134
  229.8 12.4 %collective-permute-done.1 = f32[128,1024]{1,0:T(8,128)S(1)} collective-permute-done((f32[128,1024]{1,0:T(8,128)S(1)}, f32[128,1024]{1,0:T(8,128)S(1)}, u32[]{:S(2)}, u32[]{:S(2)}) %collective-permute-start.1) | collective-permute-done | bytes 524320 | tf_op jit(solution)/shard_map/ppermute | solution.py:147
  245.1 3.9 maximum_bitcast_fusion
  249.0 15.5 %fusion.54 = f32[512,2,4,128]{3,0,2,1:T(8,128)S(1)} fusion(f32[1,4,128,2048]{3,2,1,0:T(8,128)} %get-tuple-element.561, f32[1,4,128,2048]{3,2,1,0:T(8,128)} %get-tuple-element.560, f32[512,1024]{1,0:T(8,128)S(1)} %copy-done.2, f32[512,1024]{1,0:T(8,128)S(1)} %get-tuple-element.572), kind=kOutput, calls=%fused_computation.86 | convolution fusion | flops 12888047616 | bytes 14680064 | tf_op jit(solution)/shard_map/dot_general | solution.py:163
  265.8 51.6 %all_to_all.67 = f32[512,2,4,128]{3,2,1,0:T(4,128)S(1)} all-to-all(f32[512,2,4,128]{3,2,1,0:T(4,128)S(1)} %copy.63), channel_id=1, replica_groups=mesh['space'=8,'kern'=4] {'space'}, dimensions={0} | all-to-all | bytes 4194304 | tf_op jit(solution)/shard_map/all_to_all | solution.py:165
  325.8 4.7 copy.65
  330.5 5.3 reshape.168
  335.8 8.9 %fusion.71 = f32[512,512]{1,0:T(8,128)S(1)} fusion(f32[512,2048]{1,0:T(8,128)} %reshape.168, f32[512,1024]{1,0:T(8,128)} %get-tuple-element.573, f32[512,1024]{1,0:T(8,128)S(1)} %get-tuple-element.572), kind=kOutput, calls=%fused_computation.117 | convolution fusion | flops 6443499520 | bytes 9437184 | tf_op jit(solution)/shard_map/dot_general | solution.py:175
  347.0 17.9 %reduce-scatter.3.cloned.1.call-done = f32[16,512]{1,0:T(8,128)} async-done(((f32[64,512]{1,0:T(8,128)}), f32[16,512]{1,0:T(8,128)}) %reduce-scatter.3.cloned.1.call-update) | async-done | bytes 32784 | tf_op jit(solution)/shard_map/reduce_scatter | solution.py:181
  365.7 22.0 %reduce-scatter.5.cloned.1.call-done = f32[16,512]{1,0:T(8,128)} async-done(((f32[64,512]{1,0:T(8,128)}), f32[16,512]{1,0:T(8,128)}) %reduce-scatter.5.cloned.1.call-update) | async-done | bytes 32784 | tf_op jit(solution)/shard_map/reduce_scatter | solution.py:182
  388.5 49.1 %while.64 = (s32[]{:T(128)}, f32[32,4096]{1,0:T(8,128)S(1)}, f32[32,1024]{1,0:T(8,128)S(1)}, s32[]{:T(128)}, s32[]{:T(128)}, /*index=5*/s32[]{:T(128)}, s32[]{:T(128)}) while((s32[]{:T(128)}, f32[32,4096]{1,0:T(8,128)S(1)}, f32[32,1024]{1,0:T(8,128)S(1)}, s32[]{:T(128)}, s32[]{:T(128)}, /*index=5*/s32[]{:T(128)}, ...), condition=%wide.region_10.11_spmd.clone, body=%wide.region_9.10_spmd.clone.sunk | while | flops 412616192 | bytes 8663171 | solution.py:83
  388.8 8.3 %fusion.108 = (f32[1024,512]{1,0:T(8,128)S(1)}, f32[1024,512]{1,0:T(8,128)S(1)}) fusion(s32[512]{0:T(512)S(1)} %iota_add_fusion.13, s32[1024]{0:T(1024)S(1)} %iota_add_fusion.14), kind=kLoop, calls=%fused_computation.20.clone.1 | loop fusion | flops 7864320 | bytes 4200448 | tf_op jit(solution)/shard_map/while/body/eval_jaxpr/cos | solution.py:27
  401.0 8.3 %fusion.108 = (f32[1024,512]{1,0:T(8,128)S(1)}, f32[1024,512]{1,0:T(8,128)S(1)}) fusion(s32[512]{0:T(512)S(1)} %iota_add_fusion.13, s32[1024]{0:T(1024)S(1)} %iota_add_fusion.14), kind=kLoop, calls=%fused_computation.20.clone.1 | loop fusion | flops 7864320 | bytes 4200448 | tf_op jit(solution)/shard_map/while/body/eval_jaxpr/cos | solution.py:27
  413.2 8.3 %fusion.108 = (f32[1024,512]{1,0:T(8,128)S(1)}, f32[1024,512]{1,0:T(8,128)S(1)}) fusion(s32[512]{0:T(512)S(1)} %iota_add_fusion.13, s32[1024]{0:T(1024)S(1)} %iota_add_fusion.14), kind=kLoop, calls=%fused_computation.20.clone.1 | loop fusion | flops 7864320 | bytes 4200448 | tf_op jit(solution)/shard_map/while/body/eval_jaxpr/cos | solution.py:27
  425.5 8.3 %fusion.108 = (f32[1024,512]{1,0:T(8,128)S(1)}, f32[1024,512]{1,0:T(8,128)S(1)}) fusion(s32[512]{0:T(512)S(1)} %iota_add_fusion.13, s32[1024]{0:T(1024)S(1)} %iota_add_fusion.14), kind=kLoop, calls=%fused_computation.20.clone.1 | loop fusion | flops 7864320 | bytes 4200448 | tf_op jit(solution)/shard_map/while/body/eval_jaxpr/cos | solution.py:27
  437.7 4.3 copy.70
  442.0 7.4 %reshape.174 = f32[8,1,16384]{2,1,0:T(1,128)S(1)} reshape(f32[4096,2,16]{2,1,0:T(2,128)} %bitcast.119) | data formatting | bytes 1048576
  449.5 19.3 %all_to_all.68 = f32[8,1,16384]{2,1,0:T(1,128)S(1)} all-to-all(f32[8,1,16384]{2,1,0:T(1,128)S(1)} %reshape.174), channel_id=1, replica_groups=mesh['space'=8,'kern'=4] {'space'}, dimensions={0} | all-to-all | bytes 1048576 | tf_op jit(solution)/shard_map/all_to_all | solution.py:185
  470.6 7.6 %reshape.175 = f32[4096,2,16]{2,1,0:T(2,128)} reshape(f32[8,16384]{1,0:T(8,128)S(1)} %reduce.1) | data formatting | bytes 1048576
  478.3 6.3 %copy.76 = f32[2,16,8,512]{3,1,2,0:T(8,128)} copy(f32[2,16,8,512]{1,0,3,2:T(2,128)} %bitcast.120) | data formatting | bytes 1048576 | tf_op jit(solution)/shard_map/all_to_all | solution.py:185
  484.6 20.8 %all-gather.2.cloned.1.call-done = f32[2,512,512]{2,1,0:T(8,128)} async-done(((f32[2,128,512]{2,1,0:T(8,128)}), f32[2,512,512]{2,1,0:T(8,128)}) %all-gather.2.cloned.1.call-update) | async-done | bytes 2097168 | tf_op jit(solution)/shard_map/all_gather | solution.py:192
  505.4 4.4 broadcast_in_dim.45.clone
  509.9 100.1 %while.65 = (s32[]{:T(128)}, f32[512,4096]{1,0:T(8,128)}, f32[1024,512]{1,0:T(8,128)}, s32[4,8]{1,0:T(4,128)S(1)}, s32[]{:T(128)}, /*index=5*/s32[]{:T(128)}, s32[]{:T(128)}, s32[]{:T(128)}) while((s32[]{:T(128)}, f32[512,4096]{1,0:T(8,128)}, f32[1024,512]{1,0:T(8,128)}, s32[4,8]{1,0:T(4,128)S(1)}, s32[]{:T(128)}, ...), condition=%wide.region_12.13_spmd.clone, body=%wide.region_11.12_spmd.clone.sunk | while | flops 6451890176 | bytes 39862572 | solution.py:97
  515.4 8.3 %fusion.112 = (f32[1024,512]{1,0:T(8,128)S(1)}, f32[1024,512]{1,0:T(8,128)S(1)}) fusion(s32[512]{0:T(512)S(1)} %sub.133, s32[1024]{0:T(1024)S(1)} %iota_add_fusion.15), kind=kLoop, calls=%fused_computation.39.clone.1 | loop fusion | flops 7864320 | bytes 4200448 | tf_op jit(solution)/shard_map/while/body/eval_jaxpr/cos | solution.py:22
  523.7 8.0 %bitcast_add_fusion.2 = f32[512,1024]{0,1:T(8,128)} fusion(f32[512,1024]{0,1:T(8,128)S(1)} %copy.92, f32[1024,512]{1,0:T(8,128)S(1)} %copy-done, f32[1024,512]{1,0:T(8,128)S(1)} %get-tuple-element.665, f32[1024,512]{1,0:T(8,128)S(1)} %get-tuple-element.666), kind=kOutput, calls=%fused_computation.37.clone.1 | convolution fusion | flops 6444023808 | bytes 10485760 | tf_op jit(solution)/shard_map/while/body/eval_jaxpr/dot_general | solution.py:93
  540.3 8.3 %fusion.112 = (f32[1024,512]{1,0:T(8,128)S(1)}, f32[1024,512]{1,0:T(8,128)S(1)}) fusion(s32[512]{0:T(512)S(1)} %sub.133, s32[1024]{0:T(1024)S(1)} %iota_add_fusion.15), kind=kLoop, calls=%fused_computation.39.clone.1 | loop fusion | flops 7864320 | bytes 4200448 | tf_op jit(solution)/shard_map/while/body/eval_jaxpr/cos | solution.py:22
  548.6 8.0 %bitcast_add_fusion.2 = f32[512,1024]{0,1:T(8,128)} fusion(f32[512,1024]{0,1:T(8,128)S(1)} %copy.92, f32[1024,512]{1,0:T(8,128)S(1)} %copy-done, f32[1024,512]{1,0:T(8,128)S(1)} %get-tuple-element.665, f32[1024,512]{1,0:T(8,128)S(1)} %get-tuple-element.666), kind=kOutput, calls=%fused_computation.37.clone.1 | convolution fusion | flops 6444023808 | bytes 10485760 | tf_op jit(solution)/shard_map/while/body/eval_jaxpr/dot_general | solution.py:93
  565.3 8.3 %fusion.112 = (f32[1024,512]{1,0:T(8,128)S(1)}, f32[1024,512]{1,0:T(8,128)S(1)}) fusion(s32[512]{0:T(512)S(1)} %sub.133, s32[1024]{0:T(1024)S(1)} %iota_add_fusion.15), kind=kLoop, calls=%fused_computation.39.clone.1 | loop fusion | flops 7864320 | bytes 4200448 | tf_op jit(solution)/shard_map/while/body/eval_jaxpr/cos | solution.py:22
  573.6 8.0 %bitcast_add_fusion.2 = f32[512,1024]{0,1:T(8,128)} fusion(f32[512,1024]{0,1:T(8,128)S(1)} %copy.92, f32[1024,512]{1,0:T(8,128)S(1)} %copy-done, f32[1024,512]{1,0:T(8,128)S(1)} %get-tuple-element.665, f32[1024,512]{1,0:T(8,128)S(1)} %get-tuple-element.666), kind=kOutput, calls=%fused_computation.37.clone.1 | convolution fusion | flops 6444023808 | bytes 10485760 | tf_op jit(solution)/shard_map/while/body/eval_jaxpr/dot_general | solution.py:93
  590.3 8.3 %fusion.112 = (f32[1024,512]{1,0:T(8,128)S(1)}, f32[1024,512]{1,0:T(8,128)S(1)}) fusion(s32[512]{0:T(512)S(1)} %sub.133, s32[1024]{0:T(1024)S(1)} %iota_add_fusion.15), kind=kLoop, calls=%fused_computation.39.clone.1 | loop fusion | flops 7864320 | bytes 4200448 | tf_op jit(solution)/shard_map/while/body/eval_jaxpr/cos | solution.py:22
  598.6 8.0 %bitcast_add_fusion.2 = f32[512,1024]{0,1:T(8,128)} fusion(f32[512,1024]{0,1:T(8,128)S(1)} %copy.92, f32[1024,512]{1,0:T(8,128)S(1)} %copy-done, f32[1024,512]{1,0:T(8,128)S(1)} %get-tuple-element.665, f32[1024,512]{1,0:T(8,128)S(1)} %get-tuple-element.666), kind=kOutput, calls=%fused_computation.37.clone.1 | convolution fusion | flops 6444023808 | bytes 10485760 | tf_op jit(solution)/shard_map/while/body/eval_jaxpr/dot_general | solution.py:93
  (139 shorter events, 120.5 us)
Async XLA Ops:
  30.4 21.7 %all-to-all-start = ((f32[2,128,512]{2,0,1:T(2,128)}), f32[2,128,512]{2,0,1:T(2,128)S(1)}, u32[]{:S(2)}, u32[]{:S(2)}) async-start(f32[2,128,512]{2,0,1:T(2,128)} %copy.57), calls=%async_computation | async-start | bytes 1048576 | tf_op jit(solution)/shard_map/all_to_all | solution.py:114
  37.6 327.3 %reduce-scatter.3.cloned.1.call-start = ((), (), s32[]{:S(2)}) async-start(), calls=%async_computation.6 | async-start | bytes 163840 | tf_op jit(solution)/shard_map/reduce_scatter | solution.py:181
  53.6 53.8 %copy-start.4 = (f32[2,4,64,512]{3,2,1,0:T(8,128)S(1)}, f32[2,4,64,512]{3,2,1,0:T(8,128)}, u32[]{:S(2)}) copy-start(f32[2,4,64,512]{3,2,1,0:T(8,128)} %param.12) | copy-start | bytes 3145732
  101.2 6.5 %copy-start.1 = (f32[512,1024]{1,0:T(8,128)S(1)}, f32[512,1024]{1,0:T(8,128)}, u32[]{:S(2)}) copy-start(f32[512,1024]{1,0:T(8,128)} %get-tuple-element.573) | copy-start | bytes 6291460
  226.1 16.2 %copy-start.5 = (s32[128,1024]{1,0:T(8,128)S(1)}, s32[128,1024]{1,0:T(8,128)}, u32[]{:S(2)}) copy-start(s32[128,1024]{1,0:T(8,128)} %param.13) | copy-start | bytes 1572868
  226.2 2.0 collective-permute-start
  228.2 14.0 %collective-permute-start.1 = (f32[128,1024]{1,0:T(8,128)S(1)}, f32[128,1024]{1,0:T(8,128)S(1)}, u32[]{:S(2)}, u32[]{:S(2)}) collective-permute-start(f32[128,1024]{1,0:T(8,128)S(1)} %fusion.87), channel_id=1, source_target_pairs={{0,2},{1,3},{2,0},{3,1},{4,6},{5,7},{6,4},{7,5},{8,10},{9,11},{10,... | collective-permute-start | bytes 1572872 | tf_op jit(solution)/shard_map/ppermute | solution.py:147
  245.1 3.9 copy-start.2
  322.7 1.9 copy-start.3
  346.2 41.4 %reduce-scatter.5.cloned.1.call-start = ((), (), s32[]{:S(2)}) async-start(), calls=%async_computation.7 | async-start | bytes 163840 | tf_op jit(solution)/shard_map/reduce_scatter | solution.py:182
  347.0 158.5 %all-gather.2.cloned.1.call-start = ((), (), s32[]{:S(2)}) async-start(), calls=%async_computation.8 | async-start | bytes 2621440 | tf_op jit(solution)/shard_map/all_gather | solution.py:192
  515.4 8.3 %copy-start = (f32[1024,512]{1,0:T(8,128)S(1)}, f32[1024,512]{1,0:T(8,128)}, u32[]{:S(2)}) copy-start(f32[1024,512]{1,0:T(8,128)} %get-tuple-element.762) | copy-start | bytes 6291460 | tf_op jit(solution)/shard_map/while
  540.3 8.3 %copy-start = (f32[1024,512]{1,0:T(8,128)S(1)}, f32[1024,512]{1,0:T(8,128)}, u32[]{:S(2)}) copy-start(f32[1024,512]{1,0:T(8,128)} %get-tuple-element.762) | copy-start | bytes 6291460 | tf_op jit(solution)/shard_map/while
  565.3 8.3 %copy-start = (f32[1024,512]{1,0:T(8,128)S(1)}, f32[1024,512]{1,0:T(8,128)}, u32[]{:S(2)}) copy-start(f32[1024,512]{1,0:T(8,128)} %get-tuple-element.762) | copy-start | bytes 6291460 | tf_op jit(solution)/shard_map/while
  590.2 8.3 %copy-start = (f32[1024,512]{1,0:T(8,128)S(1)}, f32[1024,512]{1,0:T(8,128)}, u32[]{:S(2)}) copy-start(f32[1024,512]{1,0:T(8,128)} %get-tuple-element.762) | copy-start | bytes 6291460 | tf_op jit(solution)/shard_map/while
Sparse Core Ops, SparseCore 0:
  346.3 18.5 reduce-scatter.2
  368.0 19.5 reduce-scatter.4
  484.7 20.7 all-gather.1
